TPU v7x, 256 devices: a whole 4x4x8 slice. The times are simulated.
256 devices in a mesh: dp: 8 (over x, core), tm: 8 (over z), space: 4 (over y).
Axes of the slice: x: 4, y: 4, z: 8, core: 2. Of those that a mesh axis runs over, the one named last changes fastest.
Arguments:
- latents: bfloat16 [8, 16, 8, 128, 512], P('dp', 'tm', 'space'), may hold values from -400 to 400
- owner: int32 [8, 4, 1], P('dp'), may hold values from 0 to 3; in each aligned block of 4 rows (0 to 3, 4 to 7, ..., all dimensions but the last counted through in order) at most 2 rows name the same one
- gamma: float32 [512], replicated, may hold values from 0.25 to 1.75
- beta: float32 [512], replicated, may hold values from -3 to 3
- weight: bfloat16 [512, 27, 256], P(('dp', 'tm', 'space')), may hold values from -0.0546875 to 0.0546875
- upstream: bfloat16 [8, 16, 4, 512, 256], P('dp', 'tm', 'space'), may hold values from -20 to 20
Outputs:
- dlatents: bfloat16 [8, 16, 8, 128, 512], P('dp', 'tm', 'space')
- dweight: float32 [512, 27, 256], P(('dp', 'tm', 'space'))
- dgamma: float32 [512], replicated
- dbeta: float32 [512], replicated
Inputs may be any that keep to these rules, and one draw needn't show every extreme that they name: `owner`: in every clip each of the 4 owners is named by at most 2 of the 4 tiles, and by exactly 2 in some clips.
All inputs are finite; a program needn't handle non-finite values.
Results may differ from a plain program's by a relative error of at most 0.002.
The roundings to bfloat16 on the way count: a program that leaves them out, or rounds other values in their place, can miss the bound.
Values may be sent and summed in bfloat16 or wider, within the bound.
A program may use at most 128 MiB of HBM per device.

v0:
```python
import math
import jax
import jax.numpy as jnp
from jax import lax
from jax.sharding import PartitionSpec as P

GROUPS = 32
TH = 8
TW = 16
EPS = 1e-06


def shifted(value, axis, steps):
    count = lax.axis_size(axis)
    initial, last = (max(0, -steps), min(count, count - steps))
    return lax.ppermute(value, axis, [(source, source + steps) for source in range(initial, last)])


def tap_list():
    return [(kt, ky, kx) for kt in range(3) for ky in range(3) for kx in range(3)]


def conv_grads(hidden, grads, weight, rscale):
    frames, count, cells, chans = hidden.shape
    outs_ch = grads.shape[3]
    first_dev = lax.axis_index("tm") == 0
    cache = shifted(hidden, "tm", 1)
    repeat = jnp.concatenate([hidden[:1], hidden[:1]], axis=0)
    cache = jnp.where(first_dev, repeat, cache)
    extended = jnp.concatenate([cache, hidden], axis=0).reshape(frames + 2, count, TH, TW, chans)
    padded = jnp.pad(extended, ((0, 0), (0, 0), (1, 1), (1, 1), (0, 0)))
    rows = grads.reshape(frames * count * cells, outs_ch)
    span = lax.axis_size(("dp", "tm", "space")) * weight.shape[0]
    terms = []
    for kt, ky, kx in tap_list():
        tap = padded[kt : kt + frames, :, ky : ky + TH, kx : kx + TW].reshape(
            frames * count * cells, span
        )
        terms.append(
            lax.dot_general(tap, rows, (((0,), (0,)), ((), ())), preferred_element_type=jnp.float32)
        )
    dweight = lax.psum_scatter(
        jnp.stack(terms, axis=1) * rscale, ("dp", "tm", "space"), scatter_dimension=0, tiled=True
    )
    piece = lax.all_gather(weight, ("dp", "tm", "space"), axis=0, tiled=True)
    span = piece.shape[0]
    total = jnp.zeros((frames + 2, count, TH + 2, TW + 2, span), jnp.float32)
    for index, (kt, ky, kx) in enumerate(tap_list()):
        back = lax.dot_general(
            rows, piece[:, index, :], (((1,), (1,)), ((), ())), preferred_element_type=jnp.float32
        )
        total = total.at[kt : kt + frames, :, ky : ky + TH, kx : kx + TW].add(
            back.reshape(frames, count, TH, TW, span)
        )
    dextended = total[:, :, 1 : TH + 1, 1 : TW + 1].reshape(frames + 2, count, cells, span)
    carried = shifted(dextended[:2].astype(jnp.bfloat16), "tm", -1).astype(jnp.float32)
    own_part = dextended[2:]
    own_part = own_part.at[frames - 2 :].add(carried)
    own_part = own_part.at[0].add(jnp.where(first_dev, dextended[0] + dextended[1], 0.0))
    return (own_part, dweight)


def shards(latents, owner, gamma, beta, weight, upstream):
    blocks = latents[0]
    frames, cap, cells, chans = blocks.shape
    spaces = lax.axis_size("space")
    here = lax.axis_index("space")
    per_dev = upstream.shape[2]
    outs_ch = upstream.shape[4]
    tile_ids = owner[0, :, 0]
    tiles = tile_ids.shape[0]
    width = chans // GROUPS
    hot = (tile_ids[:, None] == jnp.arange(spaces, dtype=jnp.int32)[None, :]).astype(jnp.int32)
    rank = jnp.sum((jnp.cumsum(hot, axis=0) - hot) * hot, axis=1)
    slot = tile_ids * cap + rank
    holds = slot[None, :] == (here * cap + jnp.arange(cap, dtype=jnp.int32))[:, None]
    live = jnp.any(holds, axis=1).astype(jnp.float32)
    tile_of = jnp.sum(holds.astype(jnp.int32) * jnp.arange(tiles, dtype=jnp.int32)[None, :], axis=1)
    frames_all = frames * lax.axis_size("tm")
    count = float(frames_all * tiles * cells * width)
    rscale = 1.0 / math.sqrt(lax.axis_size("dp") * frames_all * tiles * cells)
    values = blocks.astype(jnp.float32).reshape(frames, cap, cells, GROUPS, width)
    live_mask = live[None, :, None, None, None]
    total = lax.psum(jnp.sum(values * live_mask, axis=(0, 1, 2, 4)), ("tm", "space"))
    mean = total / count
    centred = values - mean[:, None]
    spread = lax.psum(jnp.sum(centred * centred * live_mask, axis=(0, 1, 2, 4)), ("tm", "space"))
    var = spread / count
    inverse = lax.rsqrt(var + EPS)
    normed = (centred * inverse[:, None]).reshape(frames, cap, cells, chans)
    act = normed * gamma + beta
    sig = jax.nn.sigmoid(act)
    hidden = (act * sig).astype(jnp.bfloat16)
    ups = upstream[0].astype(jnp.float32).reshape(frames, per_dev, TH, 2, TW, 2, outs_ch)
    pooled = jnp.sum(ups, axis=(3, 5)).reshape(frames, per_dev, cells, outs_ch).astype(jnp.bfloat16)
    all_pooled = lax.all_gather(pooled, "space", axis=1, tiled=True)
    live_slot = live[None, :, None, None] > 0.5
    grads = jnp.where(live_slot, all_pooled[:, tile_of], jnp.zeros((), jnp.bfloat16))
    dhidden, dweight = conv_grads(hidden, grads, weight, rscale)
    dact = dhidden * (sig * (1.0 + act * (1.0 - sig))) * live[None, :, None, None]
    dgamma, dbeta = lax.psum(
        (jnp.sum(dact * normed, axis=(0, 1, 2)) * rscale, jnp.sum(dact, axis=(0, 1, 2)) * rscale),
        ("dp", "tm", "space"),
    )
    dnorm = (dact * gamma).reshape(frames, cap, cells, GROUPS, width)
    ngroup = normed.reshape(frames, cap, cells, GROUPS, width)
    first_m, second_m = lax.psum(
        (jnp.sum(dnorm, axis=(0, 1, 2, 4)), jnp.sum(dnorm * ngroup, axis=(0, 1, 2, 4))),
        ("tm", "space"),
    )
    dvalues = inverse[:, None] * (
        dnorm - (first_m / count)[:, None] - ngroup * (second_m / count)[:, None]
    )
    dfull = dvalues.reshape(frames, cap, cells, chans)
    resid = jnp.pad(grads.astype(jnp.float32), ((0, 0), (0, 0), (0, 0), (0, chans - outs_ch)))
    dlatent = ((dfull + resid) * live[None, :, None, None]).astype(jnp.bfloat16)
    return (dlatent[None], dweight, dgamma, dbeta)


def solution(mesh):
    return jax.shard_map(
        shards,
        mesh=mesh,
        in_specs=(
            P("dp", "tm", "space", None, None),
            P("dp", None, None),
            P(),
            P(),
            P(("dp", "tm", "space"), None, None),
            P("dp", "tm", "space", None, None),
        ),
        out_specs=(
            P("dp", "tm", "space", None, None),
            P(("dp", "tm", "space"), None, None),
            P(),
            P(),
        ),
        check_vma=False,
    )
```

profile of v0, /device:TPU:2, one launch (start us, length us, event | category | flops | bytes accessed | tf_op | source)
XLA Modules:
  0.0 780.4 jit_solution(5624047049725243167)
XLA Ops:
  13.3 13.3 %all_gather.6 = bf16[2,4,128,256]{3,2,1,0:T(8,128)(2,1)S(1)} all-gather(bf16[2,1,128,256]{3,2,1,0:T(8,128)(2,1)S(1)} %bitcast.575), channel_id=1, replica_groups=mesh['dp'=8,'tm'=8,'space'=4] {'space'}, dimensions={1}, use_global_device_ids=true | all-gather | bytes 655360 | tf_op jit(solution)/shard_map/all_gather | solution.py:96
  29.4 78.8 %psum.42 = f32[32]{0:T(128)S(1)} all-reduce(f32[32]{0:T(128)S(1)} %reduce_sum.114), channel_id=1, replica_groups=mesh['dp'=8,'tm'=8,'space'=4] {'tm','space'}, use_global_device_ids=true, to_apply=%region_5.6 | all-reduce | flops 32 | bytes 256 | tf_op jit(solution)/shard_map/psum | solution.py:84
  110.6 22.7 %all-gather.2.cloned.1.call-done = bf16[512,27,256]{2,1,0:T(8,128)(2,1)} async-done(((bf16[2,27,256]{2,1,0:T(8,128)(2,1)}), bf16[512,27,256]{2,1,0:T(8,128)(2,1)}) %all-gather.2.cloned.1.call-update) | async-done | bytes 7077904 | tf_op jit(solution)/shard_map/all_gather | solution.py:45
  133.3 10.9 %fusion.73 = (bf16[512,1,256]{2,1,0:T(2,128)(2,1)S(1)}, bf16[512,1,256]{2,1,0:T(2,128)(2,1)S(1)}, bf16[512,1,256]{2,1,0:T(2,128)(2,1)}, bf16[512,1,256]{2,1,0:T(...) fusion(bf16[512,27,256]{2,1,0:T(8,128)(2,1)} %all-gather.2.clon, ...), kind=kLoop, calls=%fused_computation.207 | loop fusion | bytes 4194304 | tf_op jit(solution)/shard_map/slice | solution.py:50
  147.3 5.8 scatter-add.95
  155.0 5.8 scatter-add.96
  160.8 2.8 fusion.7
  165.5 5.8 scatter-add.100
  171.2 3.9 add_select_fusion
  175.1 7.1 scatter-add.101
  186.6 5.8 scatter-add.105
  192.4 21.0 %fusion.72 = (bf16[512,1,256]{2,1,0:T(2,128)(2,1)S(1)}, bf16[512,1,256]{2,1,0:T(2,128)(2,1)S(1)}, bf16[512,1,256]{2,1,0:T(2,128)(2,1)}, bf16[512,1,256]{2,1,0:T(...) fusion(bf16[512,27,256]{2,1,0:T(8,128)(2,1)} %all-gather.2.clon, ...), kind=kLoop, calls=%fused_computation.206 | loop fusion | bytes 9961472 | tf_op jit(solution)/shard_map/slice | solution.py:50
  215.1 5.8 scatter-add.106
  225.5 5.8 scatter-add.110
  233.2 5.8 scatter-add.111
  243.7 5.8 scatter-add.115
  251.4 6.0 scatter-add.116
  262.0 5.8 scatter-add.120
  269.6 5.8 scatter-add.121
  280.1 5.8 scatter-add.125
  287.8 5.8 scatter-add.126
  298.3 5.8 scatter-add.130
  306.0 5.8 scatter-add.131
  316.3 5.8 scatter-add.135
  323.9 5.8 scatter-add.136
  334.1 74.6 %psum.43 = f32[32]{0:T(128)S(1)} all-reduce(f32[32]{0:T(128)S(1)} %reduce_sum.117), channel_id=1, replica_groups=mesh['dp'=8,'tm'=8,'space'=4] {'tm','space'}, use_global_device_ids=true, to_apply=%region_8.9 | all-reduce | flops 32 | bytes 256 | tf_op jit(solution)/shard_map/psum | solution.py:87
  417.0 6.6 collective-permute-done.1
  427.1 3.1 pad_slice_fusion
  461.2 11.5 %broadcast_multiply_fusion = f32[512,27,256]{2,0,1:T(8,128)} fusion(f32[512,27,256]{2,0,1:T(8,128)} %fusion.9), kind=kLoop, calls=%fused_computation.25 | loop fusion | flops 3538944 | bytes 28311552 | tf_op jit(solution)/shard_map/mul | solution.py:43
  473.2 72.7 %all-reduce.5 = (f32[32]{0:T(128)S(1)}, f32[32]{0:T(128)S(1)}) all-reduce(f32[32]{0:T(128)S(1)} %reduce_sum.126, f32[32]{0:T(128)S(1)} %reduce_sum.123), channel_id=1, replica_groups=mesh['dp'=8,'tm'=8,'space'=4] {'tm','space'}, use_global_device_ids=true, to_apply=%region_17.18 | all-reduce | flops 64 | bytes 512 | tf_op jit(solution)/shard_map/psum | solution.py:107
  547.8 80.5 %all-reduce.4 = (f32[512]{0:T(512)}, f32[512]{0:T(512)}) all-reduce(f32[512]{0:T(512)S(1)} %get-tuple-element.442, f32[512]{0:T(512)S(1)} %get-tuple-element.441), channel_id=1, replica_groups=mesh['dp'=8,'tm'=8,'space'=4] {'dp','tm','space'}, use_global_device_ids=true, to_apply=%region_20.21 | all-reduce | flops 1024 | bytes 8192 | tf_op jit(solution)/shard_map/psum | solution.py:101
  628.2 143.5 %all-reduce.8.cloned.1.call-done = f32[512,27,256]{2,0,1:T(8,128)} async-done(((f32[512,27,256]{2,0,1:T(8,128)}), f32[512,27,256]{2,0,1:T(8,128)}) %all-reduce.8.cloned.1.call-update) | async-done | bytes 14155792
  (129 shorter events, 114.0 us)
Async XLA Ops:
  7.2 126.1 %all-gather.2.cloned.1.call-start = ((), (), s32[]{:S(2)}) async-start(), calls=%async_computation | async-start | bytes 8421376 | tf_op jit(solution)/shard_map/all_gather | solution.py:45
  8.6 763.1 %all-reduce.8.cloned.1.call-start = ((), (), s32[]{:S(2)}) async-start(), calls=%async_computation.1 | async-start | bytes 28311552
  323.9 90.0 %copy-start.1 = (f32[512]{0:T(512)S(1)}, f32[512]{0:T(512)}, u32[]{:S(2)}) copy-start(f32[512]{0:T(512)} %param.68) | copy-start | bytes 6148
  323.9 90.0 %copy-start.2 = (f32[512]{0:T(512)S(1)}, f32[512]{0:T(512)}, u32[]{:S(2)}) copy-start(f32[512]{0:T(512)} %param.69) | copy-start | bytes 6148
  332.3 80.3 %collective-permute-start = (bf16[2,2,128,512]{2,3,1,0:T(8,128)(2,1)}, bf16[2,2,128,512]{2,3,1,0:T(8,128)(2,1)}, u32[]{:S(2)}, u32[]{:S(2)}) collective-permute-start(bf16[2,2,128,512]{2,3,1,0:T(8,128)(2,1)} %copy.128), channel_id=1, source_target_pairs={{4,0},{8,4},{12,8},{16,12},{20,16},{24,20},{28,24},{5,1},{9,5},{13... | collective-permute-start | bytes 1572872 | tf_op jit(solution)/shard_map/ppermute | solution.py:16
  415.7 8.0 %collective-permute-start.1 = (bf16[2,2,128,512]{2,3,1,0:T(8,128)(2,1)S(1)}, bf16[2,2,128,512]{2,3,1,0:T(8,128)(2,1)S(1)}, u32[]{:S(2)}, u32[]{:S(2)}) collective-permute-start(bf16[2,2,128,512]{2,3,1,0:T(8,128)(2,1)S(1)} %get-tuple-element.436), channel_id=1, source_target_pairs={{0,4},{4,8},{8,12},{12,16},{16,20},{20,24},{24,28},{1,5},{5,9},{9,... | collective-permute-start | bytes 1572872 | tf_op jit(solution)/shard_map/ppermute | solution.py:16
  472.7 73.5 %copy-start = (f32[2,2,128,512]{2,3,1,0:T(8,128)S(1)}, f32[2,2,128,512]{2,3,1,0:T(8,128)}, u32[]{:S(2)}) copy-start(f32[2,2,128,512]{2,3,1,0:T(8,128)} %get-tuple-element.384) | copy-start | bytes 3145732
Sparse Core Ops, SparseCore 0:
  12.4 120.8 all-gather.1
  472.9 298.7 all-reduce.7
where the time goes:
time: 786 us; the launch traced here: 780 us
  blocking collectives  320 us (41%)
  waiting for transfers between devices  173 us (22%)
  local copies, waits for them, and re-layouts  159 us (20%)
  matrix products  87.1 us (11%)
  other arithmetic  24 us (3%)
  between operations  14.7 us (2%)
    unnamed x3, waiting for transfers between devices  144 us
    scatter-add x19, local copies, waits for them, and re-layouts, conv_grads(): total.at[kt:kt + frames, :, ky:ky + TH, kx:kx + TW]  108 us
    psum x1, blocking collectives, shards(): lax.psum((jnp.sum(dact * normed, axis=(0, 1, 2)) * rscale, jnp.sum(dact,...  80.5 us
    psum x1, blocking collectives, shards(): lax.psum(jnp.sum(values * live_mask, axis=(0, 1, 2, 4)), ('tm', 'space'))  78.8 us
    psum x1, blocking collectives, shards(): lax.psum(jnp.sum(centred * centred * live_mask, axis=(0, 1, 2, 4)), ('tm'...  74.6 us
    psum x1, blocking collectives, shards(): lax.psum((jnp.sum(dnorm, axis=(0, 1, 2, 4)), jnp.sum(dnorm * ngroup, axis...  72.7 us
    dot_general x27, matrix products, conv_grads(): lax.dot_general(rows, piece[:, index, :], (((1,), (1,)), ((), ())), prefe...  56.2 us
    slice x2, local copies, waits for them, and re-layouts, conv_grads(): piece[:, index, :]  31.9 us
  transfers between devices with their start and end apart: 4, of which 3 were waited for; matrix products, arithmetic and copies ran while one was open for 2% of the time, Pallas kernels for 0%

commit v1 on v0

--- a/solution.py
+++ b/solution.py
@@ -84,7 +84,8 @@
     total = lax.psum(jnp.sum(values * live_mask, axis=(0, 1, 2, 4)), ("tm", "space"))
     mean = total / count
     centred = values - mean[:, None]
-    spread = lax.psum(jnp.sum(centred * centred * live_mask, axis=(0, 1, 2, 4)), ("tm", "space"))
+    one_axis = lax.psum(jnp.sum(centred * centred * live_mask, axis=(0, 1, 2, 4)), "space")
+    spread = lax.psum(one_axis, "tm")
     var = spread / count
     inverse = lax.rsqrt(var + EPS)
     normed = (centred * inverse[:, None]).reshape(frames, cap, cells, chans)

time: 786 us -> 735 us (0.935)
  blocking collectives: 320 us -> 266 us
    psum x1 -> x2, blocking collectives: 74.6 us -> 27.3 us  [the longest x1 17.7 us: shards(): spread = lax.psum(one_axis, 'tm')]
    psum x1, blocking collectives: 80.5 us -> 72 us  [shards(): lax.psum((jnp.sum(dact * normed, axis=(0, 1, 2)) * rscale, jnp.sum(dact,...]
where the time goes in v1:
time: 735 us; the launch traced here: 728 us
  blocking collectives  266 us (36%)
  waiting for transfers between devices  175 us (24%)
  local copies, waits for them, and re-layouts  159 us (22%)
  matrix products  87.1 us (12%)
  other arithmetic  24 us (3%)
  between operations  14.7 us (2%)
    unnamed x3, waiting for transfers between devices  146 us
    scatter-add x19, local copies, waits for them, and re-layouts, conv_grads(): total.at[kt:kt + frames, :, ky:ky + TH, kx:kx + TW]  108 us
    psum x1, blocking collectives, shards(): lax.psum(jnp.sum(values * live_mask, axis=(0, 1, 2, 4)), ('tm', 'space'))  78.8 us
    psum x1, blocking collectives, shards(): lax.psum((jnp.sum(dnorm, axis=(0, 1, 2, 4)), jnp.sum(dnorm * ngroup, axis...  74.4 us
    psum x1, blocking collectives, shards(): lax.psum((jnp.sum(dact * normed, axis=(0, 1, 2)) * rscale, jnp.sum(dact,...  72 us
    dot_general x27, matrix products, conv_grads(): lax.dot_general(rows, piece[:, index, :], (((1,), (1,)), ((), ())), prefe...  56.2 us
    slice x2, local copies, waits for them, and re-layouts, conv_grads(): piece[:, index, :]  31.9 us
    dot_general x27, matrix products, conv_grads(): lax.dot_general(tap, rows, (((0,), (0,)), ((), ())), preferred_element_ty...  31 us
  transfers between devices with their start and end apart: 4, of which 3 were waited for; matrix products, arithmetic and copies ran while one was open for 2% of the time, Pallas kernels for 0%

profile of v1, /device:TPU:2, one launch (start us, length us, event | category | flops | bytes accessed | tf_op | source)
XLA Modules:
  0.0 728.5 jit_solution(17461064628854679134)
XLA Ops:
  13.3 13.3 %all_gather.6 = bf16[2,4,128,256]{3,2,1,0:T(8,128)(2,1)S(1)} all-gather(bf16[2,1,128,256]{3,2,1,0:T(8,128)(2,1)S(1)} %bitcast.575), channel_id=1, replica_groups=mesh['dp'=8,'tm'=8,'space'=4] {'space'}, dimensions={1}, use_global_device_ids=true | all-gather | bytes 655360 | tf_op jit(solution)/shard_map/all_gather | solution.py:97
  29.4 78.8 %psum.49 = f32[32]{0:T(128)S(1)} all-reduce(f32[32]{0:T(128)S(1)} %reduce_sum.114), channel_id=1, replica_groups=mesh['dp'=8,'tm'=8,'space'=4] {'tm','space'}, use_global_device_ids=true, to_apply=%region_5.6 | all-reduce | flops 32 | bytes 256 | tf_op jit(solution)/shard_map/psum | solution.py:84
  110.6 22.7 %all-gather.2.cloned.1.call-done = bf16[512,27,256]{2,1,0:T(8,128)(2,1)} async-done(((bf16[2,27,256]{2,1,0:T(8,128)(2,1)}), bf16[512,27,256]{2,1,0:T(8,128)(2,1)}) %all-gather.2.cloned.1.call-update) | async-done | bytes 7077904 | tf_op jit(solution)/shard_map/all_gather | solution.py:45
  133.3 10.9 %fusion.73 = (bf16[512,1,256]{2,1,0:T(2,128)(2,1)S(1)}, bf16[512,1,256]{2,1,0:T(2,128)(2,1)S(1)}, bf16[512,1,256]{2,1,0:T(2,128)(2,1)}, bf16[512,1,256]{2,1,0:T(...) fusion(bf16[512,27,256]{2,1,0:T(8,128)(2,1)} %all-gather.2.clon, ...), kind=kLoop, calls=%fused_computation.207 | loop fusion | bytes 4194304 | tf_op jit(solution)/shard_map/slice | solution.py:50
  147.3 5.8 scatter-add.95
  155.0 5.8 scatter-add.96
  165.5 5.8 scatter-add.100
  171.2 3.9 add_select_fusion
  175.1 7.1 scatter-add.101
  186.6 5.8 scatter-add.105
  192.4 21.0 %fusion.72 = (bf16[512,1,256]{2,1,0:T(2,128)(2,1)S(1)}, bf16[512,1,256]{2,1,0:T(2,128)(2,1)S(1)}, bf16[512,1,256]{2,1,0:T(2,128)(2,1)}, bf16[512,1,256]{2,1,0:T(...) fusion(bf16[512,27,256]{2,1,0:T(8,128)(2,1)} %all-gather.2.clon, ...), kind=kLoop, calls=%fused_computation.206 | loop fusion | bytes 9961472 | tf_op jit(solution)/shard_map/slice | solution.py:50
  215.1 5.8 scatter-add.106
  225.5 5.8 scatter-add.110
  233.2 5.8 scatter-add.111
  243.7 5.8 scatter-add.115
  251.4 6.0 scatter-add.116
  262.0 5.8 scatter-add.120
  269.6 5.8 scatter-add.121
  280.1 5.8 scatter-add.125
  287.8 5.8 scatter-add.126
  298.3 5.8 scatter-add.130
  306.0 5.8 scatter-add.131
  316.3 5.8 scatter-add.135
  323.9 5.8 scatter-add.136
  334.1 9.5 %psum.50 = f32[32]{0:T(128)S(1)} all-reduce(f32[32]{0:T(128)S(1)} %reduce_sum.117), channel_id=1, replica_groups=mesh['dp'=8,'tm'=8,'space'=4] {'space'}, use_global_device_ids=true, to_apply=%region_8.9 | all-reduce | flops 32 | bytes 256 | tf_op jit(solution)/shard_map/psum | solution.py:87
  343.7 17.7 %psum.51 = f32[32]{0:T(128)S(1)} all-reduce(f32[32]{0:T(128)S(1)} %psum.50), channel_id=1, replica_groups=mesh['dp'=8,'tm'=8,'space'=4] {'tm'}, use_global_device_ids=true, to_apply=%region_9.10 | all-reduce | flops 32 | bytes 256 | tf_op jit(solution)/shard_map/psum | solution.py:88
  369.7 6.6 collective-permute-done.1
  379.7 3.1 pad_slice_fusion
  413.9 11.5 %broadcast_multiply_fusion = f32[512,27,256]{2,0,1:T(8,128)} fusion(f32[512,27,256]{2,0,1:T(8,128)} %fusion.9), kind=kLoop, calls=%fused_computation.25 | loop fusion | flops 3538944 | bytes 28311552 | tf_op jit(solution)/shard_map/mul | solution.py:43
  425.8 74.4 %all-reduce.5 = (f32[32]{0:T(128)S(1)}, f32[32]{0:T(128)S(1)}) all-reduce(f32[32]{0:T(128)S(1)} %reduce_sum.126, f32[32]{0:T(128)S(1)} %reduce_sum.123), channel_id=1, replica_groups=mesh['dp'=8,'tm'=8,'space'=4] {'tm','space'}, use_global_device_ids=true, to_apply=%region_18.19 | all-reduce | flops 64 | bytes 512 | tf_op jit(solution)/shard_map/psum | solution.py:108
  502.1 72.0 %all-reduce.4 = (f32[512]{0:T(512)}, f32[512]{0:T(512)}) all-reduce(f32[512]{0:T(512)S(1)} %get-tuple-element.442, f32[512]{0:T(512)S(1)} %get-tuple-element.441), channel_id=1, replica_groups=mesh['dp'=8,'tm'=8,'space'=4] {'dp','tm','space'}, use_global_device_ids=true, to_apply=%region_21.22 | all-reduce | flops 1024 | bytes 8192 | tf_op jit(solution)/shard_map/psum | solution.py:102
  574.0 145.8 %all-reduce.8.cloned.1.call-done = f32[512,27,256]{2,0,1:T(8,128)} async-done(((f32[512,27,256]{2,0,1:T(8,128)}), f32[512,27,256]{2,0,1:T(8,128)}) %all-reduce.8.cloned.1.call-update) | async-done | bytes 14155792
  (130 shorter events, 116.8 us)
Async XLA Ops:
  7.2 126.1 %all-gather.2.cloned.1.call-start = ((), (), s32[]{:S(2)}) async-start(), calls=%async_computation | async-start | bytes 8421376 | tf_op jit(solution)/shard_map/all_gather | solution.py:45
  8.6 711.2 %all-reduce.8.cloned.1.call-start = ((), (), s32[]{:S(2)}) async-start(), calls=%async_computation.1 | async-start | bytes 28311552
  323.9 42.7 %copy-start.1 = (f32[512]{0:T(512)S(1)}, f32[512]{0:T(512)}, u32[]{:S(2)}) copy-start(f32[512]{0:T(512)} %param.68) | copy-start | bytes 6148
  323.9 42.7 %copy-start.2 = (f32[512]{0:T(512)S(1)}, f32[512]{0:T(512)}, u32[]{:S(2)}) copy-start(f32[512]{0:T(512)} %param.69) | copy-start | bytes 6148
  332.3 33.0 %collective-permute-start = (bf16[2,2,128,512]{2,3,1,0:T(8,128)(2,1)}, bf16[2,2,128,512]{2,3,1,0:T(8,128)(2,1)}, u32[]{:S(2)}, u32[]{:S(2)}) collective-permute-start(bf16[2,2,128,512]{2,3,1,0:T(8,128)(2,1)} %copy.128), channel_id=1, source_target_pairs={{4,0},{8,4},{12,8},{16,12},{20,16},{24,20},{28,24},{5,1},{9,5},{13... | collective-permute-start | bytes 1572872 | tf_op jit(solution)/shard_map/ppermute | solution.py:16
  368.3 8.0 %collective-permute-start.1 = (bf16[2,2,128,512]{2,3,1,0:T(8,128)(2,1)S(1)}, bf16[2,2,128,512]{2,3,1,0:T(8,128)(2,1)S(1)}, u32[]{:S(2)}, u32[]{:S(2)}) collective-permute-start(bf16[2,2,128,512]{2,3,1,0:T(8,128)(2,1)S(1)} %get-tuple-element.436), channel_id=1, source_target_pairs={{0,4},{4,8},{8,12},{12,16},{16,20},{20,24},{24,28},{1,5},{5,9},{9,... | collective-permute-start | bytes 1572872 | tf_op jit(solution)/shard_map/ppermute | solution.py:16
  425.4 75.1 %copy-start = (f32[2,2,128,512]{2,3,1,0:T(8,128)S(1)}, f32[2,2,128,512]{2,3,1,0:T(8,128)}, u32[]{:S(2)}) copy-start(f32[2,2,128,512]{2,3,1,0:T(8,128)} %get-tuple-element.384) | copy-start | bytes 3145732
Sparse Core Ops, SparseCore 0:
  12.4 120.8 all-gather.1
  425.5 294.2 all-reduce.7
